TPU v7x, 128 devices: a whole 4x4x4 slice. The times are simulated.
128 devices in a mesh: row: 8 (over z, core), col: 16 (over x, y).
Axes of the slice: x: 4, y: 4, z: 4, core: 2. Of those that a mesh axis runs over, the one named last changes fastest.
Arguments:
- features: float32 [24576, 128], P(('row', 'col')), may hold values from -6 to 6
- squared_scales: float32 [128], replicated, may hold values from 64 to 256
- noise_var: float32 [24576], P(('row', 'col')), may hold values from 0.05 to 0.5
- signal: float32 [1], replicated, may hold values from 0.5 to 2
Outputs:
- updated: float32 [24576, 24576], P('row', 'col')
- panel_out: float32 [24576, 256], P('row')
All inputs are finite; a program needn't handle non-finite values.
Results may differ from a plain program's by a relative error of at most 0.0003.
Values sent between devices are 32-bit elements; how exact they have to be, the bound alone decides.
A program may use at most 128 MiB of HBM per device.

v0:
```python
import functools
import math

import jax
import jax.numpy as jnp
from jax import lax
from jax.experimental import pallas as pl
from jax.experimental.pallas import tpu as pltpu
from jax.sharding import PartitionSpec as P

MESH = pl.DeviceIdType.MESH
F = 128
B = 256
OWN = 192
BLOCK = 200
PIECE = 24
N_ROW = 8
N_COL = 16
NB = 32
TILE = 384
STEPS = 8
COLS = 1536
HALF = 96
FOLD = math.sqrt(5.0) / math.log(2.0)
LN2 = math.log(2.0)
BF16 = jnp.bfloat16
F32 = jnp.float32


def split2(a):
    high = a.astype(BF16)
    return high, (a - high.astype(F32)).astype(BF16)


def split3(a):
    high = a.astype(BF16)
    rest = a - high.astype(F32)
    mid = rest.astype(BF16)
    return high, mid, (rest - mid.astype(F32)).astype(BF16)


def mm(a, b):
    return jnp.dot(a, b, preferred_element_type=F32)


def left_operand(scaled):
    n = scaled.shape[0]
    sq = jnp.sum(scaled * scaled, axis=1, keepdims=True)
    high, low = split2(scaled * -2.0)
    one, two, three = split3(jnp.broadcast_to(sq, (n, F)))
    lane = lax.broadcasted_iota(jnp.int32, (n, F), 1)
    extra = jnp.where(
        lane == 0,
        one.astype(F32),
        jnp.where(
            lane == 1,
            two.astype(F32),
            jnp.where(lane == 2, three.astype(F32), jnp.where(lane < 6, 1.0, 0.0)),
        ),
    ).astype(BF16)
    return jnp.concatenate([high, low, high, extra], axis=1)


def right_operand(scaled_t):
    n = scaled_t.shape[1]
    sq = jnp.sum(scaled_t * scaled_t, axis=0, keepdims=True)
    high, low = split2(scaled_t)
    one, two, three = split3(jnp.broadcast_to(sq, (F, n)))
    sub = lax.broadcasted_iota(jnp.int32, (F, n), 0)
    extra = jnp.where(
        sub < 3,
        1.0,
        jnp.where(
            sub == 3,
            one.astype(F32),
            jnp.where(
                sub == 4,
                two.astype(F32),
                jnp.where(sub == 5, three.astype(F32), 0.0),
            ),
        ),
    ).astype(BF16)
    return jnp.concatenate([high, high, low, extra], axis=0)


def matern(u2, signal):
    a = jnp.maximum(u2, 1e-30)
    u = a * lax.rsqrt(a)
    poly = signal + u * (signal * LN2 + u * (signal * (LN2 * LN2 / 3.0)))
    return poly * jnp.exp2(-u)


def pivot_noise(tile0, tile1):
    first = tile0[0:1, :]
    second = jnp.concatenate([tile0[1:2, 0:64], tile1[0:1, 0:64]], axis=1)
    return jnp.concatenate([first, second], axis=1)


def remote(src, dst, send, recv, rr, cc):
    return pltpu.make_async_remote_copy(
        src_ref=src, dst_ref=dst, send_sem=send, recv_sem=recv,
        device_id=(rr, cc), device_id_type=MESH,
    )


def loop(low, high, body):
    def step(k, carry):
        body(k)
        return carry

    lax.fori_loop(low, high, step, 0)


def eliminate(aug, w_ref, between):
    sub8 = lax.broadcasted_iota(jnp.int32, (8, F), 0)

    def block_step(step):
        between(step)
        base = pl.multiple_of(step * NB, NB)
        half = step // 4
        shift = lax.rem(F - NB * lax.rem(step, 4), F)
        group = aug[pl.ds(base, NB), pl.ds(pl.multiple_of(half * F, F), F)]
        group = pltpu.roll(group, shift, 1)
        rep = [
            [
                jnp.broadcast_to(group[8 * g:8 * g + 8, i:i + 1], (8, F)) if g >= i // 8 else None
                for g in range(4)
            ]
            for i in range(NB)
        ]
        panel = [aug[pl.ds(base + 8 * g, 8), :] for g in range(4)]
        root = []
        for j in range(NB):
            gj, sj = divmod(j, 8)
            pivot = jnp.broadcast_to(rep[j][gj][sj:sj + 1, :], (8, F))
            inverse = 1.0 / pivot
            root.append(lax.rsqrt(pivot))
            mult = [rep[j][g] * inverse if g >= gj else None for g in range(4)]
            for i in range(j + 1, NB):
                gi, si = divmod(i, 8)
                entry = jnp.broadcast_to(rep[j][gi][si:si + 1, :], (8, F))
                for g in range(gi, 4):
                    rep[i][g] = rep[i][g] - entry * mult[g]
            line = jnp.broadcast_to(panel[gj][sj:sj + 1, :], (8, 2 * B))
            for g in range(gj, 4):
                factor = mult[g]
                if g == gj:
                    factor = jnp.where(sub8 > sj, factor, 0.0)
                panel[g] = panel[g] - jnp.concatenate([factor] * 4, axis=1) * line
        out = []
        for g in range(4):
            scale_rows = root[8 * g]
            for s in range(1, 8):
                scale_rows = jnp.where(sub8 == s, root[8 * g + s], scale_rows)
            out.append(panel[g] * jnp.concatenate([scale_rows] * 4, axis=1))
        block = jnp.concatenate(out, axis=0)
        w_ref[pl.ds(base, NB), :] = block[:, B:2 * B]
        aug[...] -= jnp.dot(
            block[:, 0:B].T, block, precision=lax.Precision.HIGHEST, preferred_element_type=F32
        )

    loop(0, B // NB, block_step)


def gather_kernel(
    feat_hbm, noise_hbm, scale_hbm, signal_ref,
    rows_ref, cols_ref, piv_ref, w_ref,
    stage, zbuf, aug, noise_ref, scale_ref,
    in_sem, s1_send, s1_recv, s2_send, s2_recv, s3_send, s3_recv,
    p1_send, h0_send, h1_send, h0_recv, h1_recv,
    z_send, z_recv, xy_send, cols_recv, sib_send,
):
    r = lax.axis_index("row")
    c = lax.axis_index("col")
    z = r // 2
    core = r % 2
    x = c // 4
    y = c % 4
    sib = z * 2 + (1 - core)
    index = c % 8

    in_copies = (
        pltpu.make_async_copy(feat_hbm, zbuf.at[z, pl.ds(0, OWN), :], in_sem.at[0]),
        pltpu.make_async_copy(feat_hbm, rows_ref.at[c], in_sem.at[1]),
        pltpu.make_async_copy(noise_hbm, noise_ref, in_sem.at[2]),
        pltpu.make_async_copy(scale_hbm, scale_ref, in_sem.at[3]),
    )
    for copy in in_copies:
        copy.start()

    barrier = pltpu.get_barrier_semaphore()

    def signal_to(rr, cc):
        pl.semaphore_signal(barrier, inc=1, device_id=(rr, cc), device_id_type=MESH)

    def greet_z(k):
        signal_to(((z + k) % 4) * 2, c)
        signal_to(((z + k) % 4) * 2 + 1, c)

    loop(1, N_COL, lambda k: signal_to(r, (c + k) % N_COL))
    loop(1, 4, greet_z)
    loop(0, N_COL, lambda k: signal_to(sib, (c + k) % N_COL))

    for copy in in_copies:
        copy.wait()
    zbuf[z, OWN:BLOCK, :] = jnp.zeros((BLOCK - OWN, F), F32)
    zbuf[z, OWN:OWN + 1, :] = noise_ref[0:1, 0:F]
    zbuf[z, OWN + 1:OWN + 2, 0:64] = noise_ref[0:1, F:OWN]

    @pl.when((r == 0) & (c < 2))
    def _():
        tile = zbuf[z, OWN:BLOCK, :]
        for q in range(12):
            stage[q, 0:16, :] = zbuf[z, 16 * q:16 * q + 16, :]
            stage[q, 16:PIECE, :] = tile

    pl.semaphore_wait(barrier, 15 + 16 + 6)

    def s1_copy(q, target):
        return remote(stage.at[q], piv_ref.at[target], s1_send.at[q], s1_recv, 0, target)

    @pl.when((r == 0) & (c == 0))
    def _():
        loop(1, 12, lambda q: s1_copy(q, q).start())
        piv_ref[0] = stage[0]

    @pl.when((r == 0) & (c == 1))
    def _():
        loop(0, 4, lambda q: s1_copy(q, 12 + q).start())

    def s2_copy(k):
        return remote(piv_ref.at[c], piv_ref.at[c], s2_send.at[k], s2_recv, k, c)

    @pl.when((r == 0) & (c != 0))
    def _():
        s1_copy(0, c).wait_recv()

    @pl.when(r == 0)
    def _():
        loop(1, N_ROW, lambda k: s2_copy(k).start())

    def x_at(k):
        return ((x + k) % 4) * 4 + y

    def y_at(k):
        return x * 4 + (y + k) % 4

    def top(slot):
        return rows_ref.at[slot, pl.ds(0, HALF), :]

    def low(slot):
        return rows_ref.at[slot, pl.ds(HALF, HALF), :]

    def top_along_x(k):
        return remote(top(c), top(c), p1_send.at[k], h0_recv.at[c], r, x_at(k))

    def low_along_y(k):
        return remote(low(c), low(c), p1_send.at[4 + k], h1_recv.at[c], r, y_at(k))

    def top_along_y(i, k):
        slot = x_at(i)
        return remote(top(slot), top(slot), h0_send.at[4 * i + k], h0_recv.at[slot], r, y_at(k))

    def low_along_x(i, k):
        slot = y_at(i)
        return remote(low(slot), low(slot), h1_send.at[4 * i + k], h1_recv.at[slot], r, x_at(k))

    def first_go(k):
        top_along_x(k).start()
        low_along_y(k).start()

    loop(1, 4, first_go)

    @pl.when(r != 0)
    def _():
        s2_copy(0).wait_recv()

    def peer(k):
        return ((x + k // 4) % 4) * 4 + (y + k % 4) % 4

    def s3_copy(k, slot):
        return remote(
            piv_ref.at[slot], piv_ref.at[slot], s3_send.at[k], s3_recv.at[slot], r, peer(k)
        )

    loop(1, N_COL, lambda k: s3_copy(k, c).start())

    def z_copy(k, slot):
        return remote(
            zbuf.at[slot], zbuf.at[slot], z_send.at[k], z_recv.at[slot],
            ((z + k) % 4) * 2 + core, c,
        )

    loop(1, 4, lambda k: z_copy(k, z).start())

    def second_go(i):
        def go(k):
            top_along_y(i, k).start()
            low_along_x(i, k).start()

        loop(1, 4, go)

    second_go(0)
    for i in (1, 3, 2):
        remote(top(x_at(i)), top(x_at(i)), p1_send.at[0], h0_recv.at[x_at(i)], r, c).wait_recv()
        remote(low(y_at(i)), low(y_at(i)), p1_send.at[0], h1_recv.at[y_at(i)], r, c).wait_recv()
        second_go(i)

    loop(1, N_COL, lambda k: s3_copy(k, peer(k)).wait_recv())

    signal = signal_ref[0, 0]
    scale = lax.rsqrt(scale_ref[...]) * FOLD
    pivots = jnp.concatenate([piv_ref[p, 0:16, :] for p in range(16)], axis=0) * scale
    u2 = mm(left_operand(pivots), right_operand(pivots.T))
    row_id = lax.broadcasted_iota(jnp.int32, (B, B), 0)
    col_id = lax.broadcasted_iota(jnp.int32, (B, B), 1)
    noise = pivot_noise(piv_ref[0, 16:PIECE, :], piv_ref[12, 16:PIECE, :])
    aug[:, 0:B] = matern(u2, signal) + jnp.where(row_id == col_id, noise, 0.0)
    aug[:, B:2 * B] = jnp.where(row_id == col_id, 1.0, 0.0)

    to_row = 2 * z + index % 2

    def xy_each(k, act):
        source = (z + k) % 4
        target = 2 * (2 * source + core) + c // 8
        mine = (target == c) & (to_row == r)

        @pl.when(mine)
        def _():
            act(None, pltpu.make_async_copy(zbuf.at[source], cols_ref.at[index], cols_recv.at[index]))

        @pl.when(jnp.logical_not(mine))
        def _():
            act(
                remote(
                    zbuf.at[source], cols_ref.at[index], xy_send.at[k], cols_recv.at[index],
                    to_row, target,
                ),
                None,
            )

    def start_either(far, near):
        (far or near).start()

    def wait_far(far, near):
        if far is not None:
            far.wait_send()

    xy_each(0, start_either)

    def z_then_xy(k):
        slot = (z + k) % 4
        z_copy(k, slot).wait_recv()
        xy_each(k, start_either)

    loop(1, 4, z_then_xy)

    def sib_copy(i):
        return remote(cols_ref.at[i], cols_ref.at[i], sib_send.at[i], cols_recv.at[i], sib, c)

    def wait_cols(i):
        pltpu.make_async_copy(zbuf.at[0], cols_ref.at[i], cols_recv.at[i]).wait()

    def hand_over(k):
        i = 2 * k + core
        wait_cols(i)
        sib_copy(i).start()

    def between(step):
        @pl.when(step == B // NB - 1)
        def _():
            loop(0, 4, hand_over)

    eliminate(aug, w_ref, between)

    loop(0, 4, lambda k: wait_cols(2 * k + 1 - core))

    def rows_wait(i):
        def each(j):
            slot = x_at(i) // 4 * 4 + y_at(j) % 4

            @pl.when(j > 0)
            def _():
                remote(top(slot), top(slot), p1_send.at[0], h0_recv.at[slot], r, c).wait_recv()

            @pl.when(i > 0)
            def _():
                remote(low(slot), low(slot), p1_send.at[0], h1_recv.at[slot], r, c).wait_recv()

        loop(0, 4, each)

    loop(0, 4, rows_wait)

    def second_sent(i):
        def each(k):
            top_along_y(i, k).wait_send()
            low_along_x(i, k).wait_send()

        loop(1, 4, each)

    loop(0, 4, second_sent)

    def first_sent(k):
        top_along_x(k).wait_send()
        low_along_y(k).wait_send()
        z_copy(k, z).wait_send()

    loop(1, 4, first_sent)
    loop(1, N_COL, lambda k: s3_copy(k, c).wait_send())
    loop(0, 4, lambda k: xy_each(k, wait_far))
    loop(0, 4, lambda k: sib_copy(2 * k + core).wait_send())

    @pl.when((r == 0) & (c == 0))
    def _():
        loop(1, 12, lambda q: s1_copy(q, q).wait_send())

    @pl.when((r == 0) & (c == 1))
    def _():
        loop(0, 4, lambda q: s1_copy(q, 12 + q).wait_send())

    @pl.when(r == 0)
    def _():
        loop(1, N_ROW, lambda k: s2_copy(k).wait_send())


def gather(features, noise, scales, signal):
    vmem = pl.BlockSpec(memory_space=pltpu.VMEM)
    smem = pl.BlockSpec(memory_space=pltpu.SMEM)
    hbm = pl.BlockSpec(memory_space=pltpu.HBM)
    dma = pltpu.SemaphoreType.DMA
    return pl.pallas_call(
        gather_kernel,
        out_shape=(
            jax.ShapeDtypeStruct((N_COL, OWN, F), F32),
            jax.ShapeDtypeStruct((8, BLOCK, F), F32),
            jax.ShapeDtypeStruct((16, PIECE, F), F32),
            jax.ShapeDtypeStruct((B, B), F32),
        ),
        in_specs=[hbm, hbm, hbm, smem],
        out_specs=(vmem,) * 4,
        scratch_shapes=[
            pltpu.VMEM((12, PIECE, F), F32),
            pltpu.VMEM((4, BLOCK, F), F32),
            pltpu.VMEM((B, 2 * B), F32),
            pltpu.VMEM((1, OWN), F32),
            pltpu.VMEM((1, F), F32),
            dma((4,)), dma((12,)), dma, dma((8,)), dma, dma((16,)), dma((16,)),
            dma((8,)), dma((16,)), dma((16,)), dma((16,)), dma((16,)),
            dma((4,)), dma((4,)), dma((4,)), dma((8,)), dma((8,)),
        ],
        compiler_params=pltpu.CompilerParams(
            collective_id=0, has_side_effects=True, vmem_limit_bytes=32 * 1024 * 1024
        ),
        cost_estimate=pl.CostEstimate(flops=10**8, bytes_accessed=10**7, transcendentals=0),
    )(features, noise, scales, signal)


def update_kernel(
    rows_ref, cols_ref, piv_ref, w_ref, scale_ref, signal_ref,
    out_hbm, panel_hbm,
    right_d, right_p, right_piv, right_w, left_d, left_p, outs, panels, out_sem, panel_sem,
):
    r = lax.axis_index("row")
    c = lax.axis_index("col")
    signal = signal_ref[0, 0]
    scale = lax.rsqrt(scale_ref[...]) * FOLD
    noise = pivot_noise(piv_ref[0, 16:PIECE, :], piv_ref[12, 16:PIECE, :])

    def pair(ref, at):
        return jnp.concatenate([ref[at, 0:OWN, :], ref[at + 1, 0:OWN, :]], axis=0) * scale

    pivots = jnp.concatenate([piv_ref[p, 0:16, :] for p in range(16)], axis=0) * scale
    right_piv[...] = right_operand(pivots.T)
    left = left_operand(pivots)
    for i in range(4):
        right_d[:, TILE * i:TILE * (i + 1)] = right_operand(pair(cols_ref, 2 * i).T)
    w = w_ref[...]
    w_high, w_low = split2(w)
    wt_high, wt_low = split2(w.T)
    right_w[...] = jnp.concatenate([wt_high, wt_high, wt_low], axis=0)
    w3 = jnp.concatenate([w_high, w_low, w_high], axis=1)
    k_pc = matern(mm(left, right_d[...]), signal)
    row_id = lax.broadcasted_iota(jnp.int32, (B, COLS), 0)
    col_id = lax.broadcasted_iota(jnp.int32, (B, COLS), 1)
    line = jnp.concatenate([noise] * 6, axis=1)
    k_pc = k_pc + jnp.where((row_id == col_id) & (c == 0), line, 0.0)
    k_high, k_low = split2(k_pc)
    p_high, p_low = split2(mm(w3, jnp.concatenate([k_high, k_high, k_low], axis=0)))
    right_p[...] = jnp.concatenate([p_high, p_high, p_low], axis=0)

    def rows_of(t):
        return pl.ds(pl.multiple_of(t * TILE, TILE), TILE)

    def panel_copy(t):
        return pltpu.make_async_copy(panels.at[rows_of(t), :], panel_hbm.at[rows_of(t), :], panel_sem.at[t])

    def front(t):
        scaled = left_operand(pair(rows_ref, 2 * t))
        left_d[rows_of(t), :] = scaled
        k_rp = matern(mm(scaled, right_piv[...]), signal)
        row_id = lax.broadcasted_iota(jnp.int32, (TILE, B), 0)
        col_id = lax.broadcasted_iota(jnp.int32, (TILE, B), 1)
        k_rp = k_rp + jnp.where((row_id == col_id) & (t == 0) & (r == 0), noise, 0.0)
        k_high, k_low = split2(k_rp)
        panel = mm(jnp.concatenate([k_high, k_low, k_high], axis=1), right_w[...])
        panels[rows_of(t), :] = panel
        p_high, p_low = split2(-panel)
        left_p[rows_of(t), :] = jnp.concatenate([p_high, p_low, p_high], axis=1)
        panel_copy(t).start()

    def out_copy(t, slot):
        return pltpu.make_async_copy(outs.at[slot], out_hbm.at[rows_of(t), :], out_sem.at[slot])

    loop(0, STEPS, front)

    def main(t):
        slot = t % 2

        @pl.when(t >= 2)
        def _():
            out_copy(t - 2, slot).wait()

        outs[slot] = matern(mm(left_d[rows_of(t), :], right_d[...]), signal) + mm(
            left_p[rows_of(t), :], right_p[...]
        )

        first = t - (c % 2) * 4

        @pl.when((r == c // 2) & (first >= 0) & (first < 4))
        def _():
            at = pl.multiple_of(first * TILE, TILE)
            lines = []
            for k in range(2):
                tile = cols_ref[2 * first + k, OWN:BLOCK, :]
                lines += [tile[0:1, :], tile[1:2, 0:64]]
            line = jnp.concatenate(lines, axis=1)
            row_id = lax.broadcasted_iota(jnp.int32, (TILE, TILE), 0)
            col_id = lax.broadcasted_iota(jnp.int32, (TILE, TILE), 1)
            outs[slot, :, pl.ds(at, TILE)] += jnp.where(row_id == col_id, line, 0.0)

        out_copy(t, slot).start()

    loop(0, STEPS, main)
    loop(0, STEPS, lambda t: panel_copy(t).wait())
    out_copy(STEPS - 2, 0).wait()
    out_copy(STEPS - 1, 1).wait()


def update(rows, cols, piv, w, scales, signal):
    vmem = pl.BlockSpec(memory_space=pltpu.VMEM)
    smem = pl.BlockSpec(memory_space=pltpu.SMEM)
    hbm = pl.BlockSpec(memory_space=pltpu.HBM)
    dma = pltpu.SemaphoreType.DMA
    return pl.pallas_call(
        update_kernel,
        out_shape=(
            jax.ShapeDtypeStruct((N_COL * OWN, COLS), F32),
            jax.ShapeDtypeStruct((N_COL * OWN, B), F32),
        ),
        in_specs=[vmem, vmem, vmem, vmem, vmem, smem],
        out_specs=(hbm, hbm),
        scratch_shapes=[
            pltpu.VMEM((4 * F, COLS), BF16),
            pltpu.VMEM((3 * B, COLS), BF16),
            pltpu.VMEM((4 * F, B), BF16),
            pltpu.VMEM((3 * B, B), BF16),
            pltpu.VMEM((N_COL * OWN, 4 * F), BF16),
            pltpu.VMEM((N_COL * OWN, 3 * B), BF16),
            pltpu.VMEM((2, TILE, COLS), F32),
            pltpu.VMEM((N_COL * OWN, B), F32),
            dma((2,)), dma((STEPS,)),
        ],
        compiler_params=pltpu.CompilerParams(vmem_limit_bytes=48 * 1024 * 1024),
        cost_estimate=pl.CostEstimate(flops=12 * 10**9, bytes_accessed=25 * 10**6, transcendentals=10**7),
    )(rows, cols, piv, w, scales, signal)


def local(features, squared_scales, noise_var, signal):
    scales = squared_scales.reshape(1, F)
    signal = signal.reshape(1, 1)
    rows, cols, piv, w = gather(features, noise_var.reshape(1, OWN), scales, signal)
    return update(rows, cols, piv, w, scales, signal)


def solution(mesh):
    return jax.shard_map(
        local,
        mesh=mesh,
        in_specs=(P(("row", "col"), None), P(), P(("row", "col")), P()),
        out_specs=(P("row", "col"), P("row", None)),
        check_vma=False,
    )
```

profile of v0, /device:TPU:41, one launch (start us, length us, event | category | flops | bytes accessed | tf_op | source)
XLA Modules:
  0.0 64.3 jit_solution(21734027094845859)
XLA Ops:
  1.3 0.0 copy-start
  1.3 0.9 %copy-done = f32[192,128]{1,0:T(8,128)S(1)} copy-done((f32[192,128]{1,0:T(8,128)S(1)}, f32[192,128]{1,0:T(8,128)}, u32[]{:S(2)}) %copy-start) | copy-done | bytes 98328
  2.2 0.0 copy-start.1
  2.2 0.7 %copy-done.1 = f32[192]{0:T(256)S(1)} copy-done((f32[192]{0:T(256)S(1)}, f32[192]{0:T(256)}, u32[]{:S(2)}) %copy-start.1) | copy-done | bytes 792
  2.9 0.0 copy-start.2
  2.9 0.7 %copy-done.2 = f32[128]{0:T(128)S(1)} copy-done((f32[128]{0:T(128)S(1)}, f32[128]{0:T(128)}, u32[]{:S(2)}) %copy-start.2) | copy-done | bytes 536
  3.5 35.8 %shard_map.59 = (f32[16,192,128]{2,1,0:T(8,128)S(1)}, f32[8,200,128]{2,1,0:T(8,128)S(1)}, f32[16,24,128]{2,1,0:T(8,128)S(1)}, f32[256,256]{1,0:T(8,128)S(1)}) custom-call(f32[192,128]{1,0:T(8,128)S(1)} %copy-done, f32[1,192]{1,0:T(1,128)S(1)} %bitcast.5, f32[1,128]{1,0:T(1,128)S(1)} %bitcast.6, f32[1,1]{1,0:T(1,128)} %bitcast.3.signal_ref), custom_call_target="tpu_custom_call" | custom-call | flops 100000000 | bytes 10000000 | tf_op jit(solution)/shard_map/pallas_call | solution.py:431
  39.4 0.0 copy-start.3
  39.4 0.6 %copy-done.3 = f32[128]{0:T(128)S(1)} copy-done((f32[128]{0:T(128)S(1)}, f32[128]{0:T(128)}, u32[]{:S(2)}) %copy-start.3) | copy-done | bytes 536
  40.0 24.2 %shard_map.60 = (f32[3072,1536]{1,0:T(8,128)}, f32[3072,256]{1,0:T(8,128)}) custom-call(f32[16,192,128]{2,1,0:T(8,128)S(1)} %get-tuple-element.6.rows_ref, f32[8,200,128]{2,1,0:T(8,128)S(1)} %get-tuple-element.7.cols_ref, f32[16,24,128]{2,1,0:T(8,128)S(1)} %get-tuple-element.8.piv_ref, f32[256,256]{1,0:T(8,128)S(1)} %get-tuple-element.9.w_ref, ...), custom_call_target="tpu_custom_call" | custom-call | flops 12000000000 | bytes 25000000 | tf_op jit(solution)/shard_map/pallas_call | solution.py:554
Async XLA Ops:
  1.3 0.9 %copy-start = (f32[192,128]{1,0:T(8,128)S(1)}, f32[192,128]{1,0:T(8,128)}, u32[]{:S(2)}) copy-start(f32[192,128]{1,0:T(8,128)} %feat_hbm.1) | copy-start | bytes 294916
  2.2 0.7 %copy-start.1 = (f32[192]{0:T(256)S(1)}, f32[192]{0:T(256)}, u32[]{:S(2)}) copy-start(f32[192]{0:T(256)} %param.6) | copy-start | bytes 2308
  2.9 0.7 %copy-start.2 = (f32[128]{0:T(128)S(1)}, f32[128]{0:T(128)}, u32[]{:S(2)}) copy-start(f32[128]{0:T(128)} %param.5) | copy-start | bytes 1540
  39.4 0.7 %copy-start.3 = (f32[128]{0:T(128)S(1)}, f32[128]{0:T(128)}, u32[]{:S(2)}) copy-start(f32[128]{0:T(128)} %param.5) | copy-start | bytes 1540
where the time goes:
time: 64.4 us; the launch traced here: 64.3 us
  Pallas kernels  60.1 us (93%)
  local copies, waits for them, and re-layouts  2.87 us (4%)
  between operations  1.3 us (2%)
    pallas_call x1, Pallas kernels, gather(): pl.pallas_call(gather_kernel, out_shape=(jax.ShapeDtypeStruct((N_COL, OWN...  35.8 us
    pallas_call x1, Pallas kernels, update(): pl.pallas_call(update_kernel, out_shape=(jax.ShapeDtypeStruct((N_COL * OW...  24.2 us
    unnamed x8, local copies, waits for them, and re-layouts  2.87 us

commit v1 on v0

v1 whole, which is shorter than its diff:
```python
import functools
import math

import jax
import jax.numpy as jnp
from jax import lax
from jax.experimental import pallas as pl
from jax.experimental.pallas import tpu as pltpu
from jax.sharding import PartitionSpec as P

MESH = pl.DeviceIdType.MESH
F = 128
B = 256
OWN = 192
BLOCK = 200
PIECE = 24
N_ROW = 8
N_COL = 16
NB = 32
TILE = 384
STEPS = 8
COLS = 1536
HALF = 96
CHUNK = 512
SPANS = ((0, 512), (512, 1024), (1024, 1536), (1536, 1792))
FOLD = math.sqrt(5.0) / math.log(2.0)
LN2 = math.log(2.0)
BF16 = jnp.bfloat16
F32 = jnp.float32


def split2(a):
    high = a.astype(BF16)
    return high, (a - high.astype(F32)).astype(BF16)


def split3(a):
    high = a.astype(BF16)
    rest = a - high.astype(F32)
    mid = rest.astype(BF16)
    return high, mid, (rest - mid.astype(F32)).astype(BF16)


def mm(a, b):
    return jnp.dot(a, b, preferred_element_type=F32)


def left_parts(scaled):
    high, low = split2(scaled)
    return high, low, 0.25 * jnp.sum(scaled * scaled, axis=1, keepdims=True)


def left_ones(n):
    return jnp.where(lax.broadcasted_iota(jnp.int32, (n, F), 1) < 3, 1.0, 0.0).astype(BF16)


def right_operand(scaled_t):
    n = scaled_t.shape[1]
    sq = -jnp.sum(scaled_t * scaled_t, axis=0, keepdims=True)
    high, low = split2(scaled_t)
    one, two, three = (part.astype(F32) for part in split3(sq))
    sub = lax.broadcasted_iota(jnp.int32, (16, n), 0)
    extra = jnp.where(sub == 0, one, jnp.where(sub == 1, two, jnp.where(sub == 2, three, 0.0)))
    return jnp.concatenate(
        [high, high, low, extra.astype(BF16), jnp.zeros((F - 16, n), BF16)], axis=0
    )


def kernel_values(scaled2, right, signal):
    high, low, sq = left_parts(scaled2)
    left = jnp.concatenate([high, low, high, left_ones(scaled2.shape[0])], axis=1)
    return matern(sq - mm(left, right), signal)


def eye(n):
    return lax.broadcasted_iota(jnp.int32, (n, n), 0) == lax.broadcasted_iota(jnp.int32, (n, n), 1)


def rows_of(t):
    return pl.ds(pl.multiple_of(t * TILE, TILE), TILE)


def matern(u2, signal):
    a = jnp.maximum(u2, 1e-30)
    u = a * lax.rsqrt(a)
    poly = signal + u * (signal * LN2 + u * (signal * (LN2 * LN2 / 3.0)))
    return poly * jnp.exp2(-u)


def pivot_noise(tile0, tile1):
    first = tile0[0:1, :]
    second = jnp.concatenate([tile0[1:2, 0:64], tile1[0:1, 0:64]], axis=1)
    return jnp.concatenate([first, second], axis=1)


def remote(src, dst, send, recv, rr, cc):
    return pltpu.make_async_remote_copy(
        src_ref=src, dst_ref=dst, send_sem=send, recv_sem=recv,
        device_id=(rr, cc), device_id_type=MESH,
    )


def loop(low, high, body):
    def step(k, carry):
        body(k)
        return carry

    lax.fori_loop(low, high, step, 0)


def eliminate(aug, w_ref, between):
    sub8 = lax.broadcasted_iota(jnp.int32, (8, F), 0)

    def block_step(step):
        between(step)
        base = pl.multiple_of(step * NB, NB)
        half = step // 4
        shift = lax.rem(F - NB * lax.rem(step, 4), F)
        group = aug[pl.ds(base, NB), pl.ds(pl.multiple_of(half * F, F), F)]
        group = pltpu.roll(group, shift, 1)
        rep = [
            [
                jnp.broadcast_to(group[8 * g:8 * g + 8, i:i + 1], (8, F)) if g >= i // 8 else None
                for g in range(4)
            ]
            for i in range(NB)
        ]
        panel = [aug[pl.ds(base + 8 * g, 8), :] for g in range(4)]
        root = []
        for j in range(NB):
            gj, sj = divmod(j, 8)
            pivot = jnp.broadcast_to(rep[j][gj][sj:sj + 1, :], (8, F))
            inverse = 1.0 / pivot
            root.append(lax.rsqrt(pivot))
            mult = [rep[j][g] * inverse if g >= gj else None for g in range(4)]
            for i in range(j + 1, NB):
                gi, si = divmod(i, 8)
                entry = jnp.broadcast_to(rep[j][gi][si:si + 1, :], (8, F))
                for g in range(gi, 4):
                    rep[i][g] = rep[i][g] - entry * mult[g]
            line = jnp.broadcast_to(panel[gj][sj:sj + 1, :], (8, 2 * B))
            for g in range(gj, 4):
                factor = mult[g]
                if g == gj:
                    factor = jnp.where(sub8 > sj, factor, 0.0)
                panel[g] = panel[g] - jnp.concatenate([factor] * 4, axis=1) * line
        out = []
        for g in range(4):
            scale_rows = root[8 * g]
            for s in range(1, 8):
                scale_rows = jnp.where(sub8 == s, root[8 * g + s], scale_rows)
            out.append(panel[g] * jnp.concatenate([scale_rows] * 4, axis=1))
        block = jnp.concatenate(out, axis=0)
        w_ref[pl.ds(base, NB), :] = block[:, B:2 * B]
        aug[...] -= jnp.dot(
            block[:, 0:B].T, block, precision=lax.Precision.HIGHEST, preferred_element_type=F32
        )

    loop(0, B // NB, block_step)


def build_kernel(
    feat_hbm, noise_hbm, scale_hbm, signal_ref,
    k_ref, k_pc_ref, w_ref,
    rows_ref, cols_ref, piv_ref, stage, tail, zbuf, aug, noise_ref, scale_ref,
    right_d, left_d,
    in_sem, s1_send, s1_recv, s2_send, s2_recv, s3_send, s3_recv, tail_send, tail_recv,
    w1_send, w1_recv, w2_send, w2_recv, w3_send, w3_recv,
    p1_send, h0_send, h1_send, h0_recv, h1_recv,
    z_send, z_recv, xy_send, cols_recv, sib_send,
):
    r = lax.axis_index("row")
    c = lax.axis_index("col")
    z = r // 2
    core = r % 2
    x = c // 4
    y = c % 4
    sib = z * 2 + (1 - core)
    index = c % 8
    root = (r == 0) & (c == 0)

    in_copies = (
        pltpu.make_async_copy(feat_hbm, zbuf.at[z, pl.ds(0, OWN), :], in_sem.at[0]),
        pltpu.make_async_copy(feat_hbm, rows_ref.at[c], in_sem.at[1]),
        pltpu.make_async_copy(noise_hbm, noise_ref, in_sem.at[2]),
        pltpu.make_async_copy(scale_hbm, scale_ref, in_sem.at[3]),
    )
    for copy in in_copies:
        copy.start()

    barrier = pltpu.get_barrier_semaphore()

    def signal_to(rr, cc):
        pl.semaphore_signal(barrier, inc=1, device_id=(rr, cc), device_id_type=MESH)

    def greet_z(k):
        signal_to(((z + k) % 4) * 2, c)
        signal_to(((z + k) % 4) * 2 + 1, c)

    loop(1, N_COL, lambda k: signal_to(r, (c + k) % N_COL))
    loop(1, 4, greet_z)
    loop(0, N_COL, lambda k: signal_to(sib, (c + k) % N_COL))

    for copy in in_copies:
        copy.wait()
    zbuf[z, OWN:BLOCK, :] = jnp.zeros((BLOCK - OWN, F), F32)
    zbuf[z, OWN:OWN + 1, :] = noise_ref[0:1, 0:F]
    zbuf[z, OWN + 1:OWN + 2, 0:64] = noise_ref[0:1, F:OWN]

    @pl.when((r == 0) & (c < 2))
    def _():
        tile = zbuf[z, OWN:BLOCK, :]
        for q in range(12):
            stage[q, 0:16, :] = zbuf[z, 16 * q:16 * q + 16, :]
            stage[q, 16:PIECE, :] = tile

    pl.semaphore_wait(barrier, 15 + 16 + 6)

    tail_copy = remote(stage.at[pl.ds(0, 4)], tail, tail_send, tail_recv, 0, 0)

    def s1_copy(q, target):
        return remote(stage.at[q], piv_ref.at[target], s1_send.at[q], s1_recv, 0, target)

    @pl.when(root)
    def _():
        loop(1, 12, lambda q: s1_copy(q, q).start())
        piv_ref[0] = stage[0]

    @pl.when((r == 0) & (c == 1))
    def _():
        tail_copy.start()
        loop(0, 4, lambda q: s1_copy(q, 12 + q).start())

    def x_at(k):
        return ((x + k) % 4) * 4 + y

    def y_at(k):
        return x * 4 + (y + k) % 4

    def top(slot):
        return rows_ref.at[slot, pl.ds(0, HALF), :]

    def bottom(slot):
        return rows_ref.at[slot, pl.ds(HALF, HALF), :]

    def top_along_x(k):
        return remote(top(c), top(c), p1_send.at[k], h0_recv.at[c], r, x_at(k))

    def bottom_along_y(k):
        return remote(bottom(c), bottom(c), p1_send.at[4 + k], h1_recv.at[c], r, y_at(k))

    def top_along_y(i, k):
        slot = x_at(i)
        return remote(top(slot), top(slot), h0_send.at[4 * i + k], h0_recv.at[slot], r, y_at(k))

    def bottom_along_x(i, k):
        slot = y_at(i)
        return remote(bottom(slot), bottom(slot), h1_send.at[4 * i + k], h1_recv.at[slot], r, x_at(k))

    def wait_top(slot):
        remote(top(slot), top(slot), p1_send.at[0], h0_recv.at[slot], r, c).wait_recv()

    def wait_bottom(slot):
        remote(bottom(slot), bottom(slot), p1_send.at[0], h1_recv.at[slot], r, c).wait_recv()

    def z_copy(k, slot):
        return remote(
            zbuf.at[slot], zbuf.at[slot], z_send.at[k], z_recv.at[slot],
            ((z + k) % 4) * 2 + core, c,
        )

    to_row = 2 * z + index % 2

    def xy_each(k, act_near, act_far):
        source = (z + k) % 4
        target = 2 * (2 * source + core) + c // 8
        mine = (target == c) & (to_row == r)

        @pl.when(mine)
        def _():
            act_near(zbuf.at[source], cols_ref.at[index], cols_recv.at[index])

        @pl.when(jnp.logical_not(mine))
        def _():
            act_far(
                remote(
                    zbuf.at[source], cols_ref.at[index], xy_send.at[k], cols_recv.at[index],
                    to_row, target,
                )
            )

    def xy_go(k):
        xy_each(
            k,
            lambda src, dst, sem: pltpu.make_async_copy(src, dst, sem).start(),
            lambda copy: copy.start(),
        )

    def first_go(k):
        top_along_x(k).start()
        bottom_along_y(k).start()

    def second_go(i):
        def go(k):
            top_along_y(i, k).start()
            bottom_along_x(i, k).start()

        loop(1, 4, go)

    loop(1, 4, first_go)
    loop(1, 4, lambda k: z_copy(k, z).start())
    xy_go(0)
    second_go(0)
    for i in (1, 3, 2):
        wait_top(x_at(i))
        wait_bottom(y_at(i))
        second_go(i)

    def s2_copy(k):
        return remote(piv_ref.at[c], piv_ref.at[c], s2_send.at[k], s2_recv, k, c)

    @pl.when((r == 0) & (c != 0))
    def _():
        s1_copy(0, c).wait_recv()

    @pl.when(r == 0)
    def _():
        loop(1, N_ROW, lambda k: s2_copy(k).start())

    def z_then_xy(k):
        z_copy(k, (z + k) % 4).wait_recv()
        xy_go(k)

    loop(1, 4, z_then_xy)

    @pl.when(r != 0)
    def _():
        s2_copy(0).wait_recv()

    def peer(k):
        return ((x + k // 4) % 4) * 4 + (y + k % 4) % 4

    def s3_copy(k, slot):
        return remote(
            piv_ref.at[slot], piv_ref.at[slot], s3_send.at[k], s3_recv.at[slot], r, peer(k)
        )

    loop(1, N_COL, lambda k: s3_copy(k, c).start())

    def sib_copy(i):
        return remote(cols_ref.at[i], cols_ref.at[i], sib_send.at[i], cols_recv.at[i], sib, c)

    def wait_cols(i):
        pltpu.make_async_copy(zbuf.at[0], cols_ref.at[i], cols_recv.at[i]).wait()

    def hand_over(k):
        i = 2 * k + core
        wait_cols(i)
        sib_copy(i).start()

    def w_piece(p):
        return w_ref.at[pl.ds(pl.multiple_of(16 * p, 16), 16), :]

    def w1_copy(p):
        return remote(w_piece(p), w_piece(p), w1_send.at[p], w1_recv, 0, p)

    def w2_copy(k):
        return remote(w_piece(c), w_piece(c), w2_send.at[k], w2_recv, k, c)

    def w3_copy(k, p):
        return remote(w_piece(p), w_piece(p), w3_send.at[k], w3_recv.at[p], r, peer(k))

    def w3_each(k, act):
        @pl.when((r != 0) | (peer(k) != 0))
        def _():
            act(w3_copy(k, c))

    def w3_go(k):
        w3_each(k, lambda copy: copy.start())

    signal = signal_ref[0, 0]
    scale = lax.rsqrt(scale_ref[...]) * FOLD

    @pl.when(root)
    def _():
        tail_copy.wait_recv()
        pivots = jnp.concatenate(
            [zbuf[0, 0:OWN, :]] + [tail[q, 0:16, :] for q in range(4)], axis=0
        ) * scale
        diagonal = pivot_noise(stage[0, 16:PIECE, :], tail[0, 16:PIECE, :])
        block = kernel_values(2.0 * pivots, right_operand(pivots.T), signal)
        aug[:, 0:B] = block + jnp.where(eye(B), diagonal, 0.0)
        aug[:, B:2 * B] = jnp.where(eye(B), 1.0, 0.0)

        def between(step):
            @pl.when(step == 5)
            def _():
                loop(0, 4, hand_over)

        eliminate(aug, w_ref, between)
        loop(1, N_COL, lambda p: w1_copy(p).start())

    @pl.when(jnp.logical_not(root))
    def _():
        loop(0, 4, hand_over)

    loop(1, N_COL, lambda k: s3_copy(k, peer(k)).wait_recv())
    loop(0, 4, lambda k: wait_cols(2 * k + 1 - core))

    pivots = jnp.concatenate([piv_ref[p, 0:16, :] for p in range(16)], axis=0) * scale
    noise = pivot_noise(piv_ref[0, 16:PIECE, :], piv_ref[12, 16:PIECE, :])
    right_d[:, COLS:COLS + B] = right_operand(pivots.T)
    for i in range(4):
        pair = jnp.concatenate([cols_ref[2 * i, 0:OWN, :], cols_ref[2 * i + 1, 0:OWN, :]], axis=0)
        right_d[:, TILE * i:TILE * (i + 1)] = right_operand((pair * scale).T)
    k_pc_ref[...] = kernel_values(2.0 * pivots, right_d[:, 0:COLS], signal)

    @pl.when(c == 0)
    def _():
        k_pc_ref[:, 0:B] += jnp.where(eye(B), noise, 0.0)

    left_d[:, 3 * F:4 * F] = left_ones(TILE)

    def tile(k):
        t = (c // 2 + k) % STEPS

        @pl.when((k == 2) & (r == 0))
        def _():
            @pl.when(c != 0)
            def _():
                w1_copy(c).wait_recv()

            loop(1, N_ROW, lambda to: w2_copy(to).start())
            loop(1, N_COL, w3_go)

        @pl.when((k == 4) & (r != 0))
        def _():
            w2_copy(0).wait_recv()
            loop(1, N_COL, w3_go)

        for m in range(2):
            slot = 2 * t + m

            @pl.when(slot % 4 != y)
            def _():
                wait_top(slot)

            @pl.when(slot // 4 != x)
            def _():
                wait_bottom(slot)

        pair = jnp.concatenate([rows_ref[2 * t], rows_ref[2 * t + 1]], axis=0)
        high, low, sq = left_parts(pair * (scale * 2.0))
        left_d[:, 0:F] = high
        left_d[:, F:2 * F] = low
        left_d[:, 2 * F:3 * F] = high
        for low_at, high_at in SPANS:
            u2 = sq - mm(left_d[...], right_d[:, low_at:high_at])
            k_ref[rows_of(t), low_at:high_at] = matern(u2, signal)

        first = t - (c % 2) * 4

        @pl.when((r == c // 2) & (first >= 0) & (first < 4))
        def _():
            at = pl.multiple_of(first * TILE, TILE)
            lines = []
            for m in range(2):
                noise_tile = cols_ref[2 * first + m, OWN:BLOCK, :]
                lines += [noise_tile[0:1, :], noise_tile[1:2, 0:64]]
            line = jnp.concatenate(lines, axis=1)
            k_ref[rows_of(t), pl.ds(at, TILE)] += jnp.where(eye(TILE), line, 0.0)

    loop(0, STEPS, tile)

    @pl.when(r == 0)
    def _():
        k_ref[0:B, COLS:COLS + B] += jnp.where(eye(B), noise, 0.0)

    @pl.when(jnp.logical_not(root))
    def _():
        loop(1, N_COL, lambda k: w3_copy(k, peer(k)).wait_recv())

    loop(1, N_COL, lambda k: w3_each(k, lambda copy: copy.wait_send()))

    def second_sent(i):
        def each(k):
            top_along_y(i, k).wait_send()
            bottom_along_x(i, k).wait_send()

        loop(1, 4, each)

    loop(0, 4, second_sent)

    def first_sent(k):
        top_along_x(k).wait_send()
        bottom_along_y(k).wait_send()
        z_copy(k, z).wait_send()

    loop(1, 4, first_sent)
    loop(1, N_COL, lambda k: s3_copy(k, c).wait_send())
    loop(0, 4, lambda k: xy_each(k, lambda src, dst, sem: None, lambda copy: copy.wait_send()))
    loop(0, 4, lambda k: sib_copy(2 * k + core).wait_send())

    @pl.when(root)
    def _():
        loop(1, 12, lambda q: s1_copy(q, q).wait_send())
        loop(1, N_COL, lambda p: w1_copy(p).wait_send())

    @pl.when((r == 0) & (c == 1))
    def _():
        tail_copy.wait_send()
        loop(0, 4, lambda q: s1_copy(q, 12 + q).wait_send())

    @pl.when(r == 0)
    def _():
        loop(1, N_ROW, lambda k: s2_copy(k).wait_send())
        loop(1, N_ROW, lambda k: w2_copy(k).wait_send())


def build(features, noise, scales, signal):
    vmem = pl.BlockSpec(memory_space=pltpu.VMEM)
    smem = pl.BlockSpec(memory_space=pltpu.SMEM)
    hbm = pl.BlockSpec(memory_space=pltpu.HBM)
    dma = pltpu.SemaphoreType.DMA
    return pl.pallas_call(
        build_kernel,
        out_shape=(
            pltpu.VMEM((N_COL * OWN, COLS + B), F32),
            pltpu.VMEM((B, COLS), F32),
            jax.ShapeDtypeStruct((B, B), F32),
        ),
        in_specs=[hbm, hbm, hbm, smem],
        out_specs=(vmem,) * 3,
        scratch_shapes=[
            pltpu.VMEM((N_COL, OWN, F), F32),
            pltpu.VMEM((8, BLOCK, F), F32),
            pltpu.VMEM((16, PIECE, F), F32),
            pltpu.VMEM((12, PIECE, F), F32),
            pltpu.VMEM((4, PIECE, F), F32),
            pltpu.VMEM((4, BLOCK, F), F32),
            pltpu.VMEM((B, 2 * B), F32),
            pltpu.VMEM((1, OWN), F32),
            pltpu.VMEM((1, F), F32),
            pltpu.VMEM((4 * F, COLS + B), BF16),
            pltpu.VMEM((TILE, 4 * F), BF16),
            dma((4,)), dma((12,)), dma, dma((8,)), dma, dma((16,)), dma((16,)), dma, dma,
            dma((16,)), dma, dma((8,)), dma, dma((16,)), dma((16,)),
            dma((8,)), dma((16,)), dma((16,)), dma((16,)), dma((16,)),
            dma((4,)), dma((4,)), dma((4,)), dma((8,)), dma((8,)),
        ],
        compiler_params=pltpu.CompilerParams(
            collective_id=0, has_side_effects=True, vmem_limit_bytes=28 * 1024 * 1024
        ),
        cost_estimate=pl.CostEstimate(flops=10**9, bytes_accessed=10**7, transcendentals=0),
    )(features, noise, scales, signal)


def apply_kernel(
    k_ref, k_pc_ref, w_ref,
    out_hbm, panel_hbm,
    right_p, right_w, left_p, panels, outs,
    out_sem, panel_sem,
):
    w = w_ref[...]
    wt_high, wt_low = split2(w.T)
    right_w[...] = jnp.concatenate([wt_high, wt_high, wt_low], axis=0)

    w_high, w_low = split2(w)
    left_w = jnp.concatenate([w_high, w_low, w_high], axis=1)
    for i in range(COLS // CHUNK):
        span = slice(CHUNK * i, CHUNK * (i + 1))
        k_high, k_low = split2(k_pc_ref[:, span])
        p_high, p_low = split2(mm(left_w, jnp.concatenate([k_high, k_high, k_low], axis=0)))
        right_p[0:B, span] = p_high
        right_p[B:2 * B, span] = p_high
        right_p[2 * B:3 * B, span] = p_low

    def panel_copy(t):
        return pltpu.make_async_copy(
            panels.at[rows_of(t), :], panel_hbm.at[rows_of(t), :], panel_sem.at[t]
        )

    def panel_tile(t):
        k_high, k_low = split2(k_ref[rows_of(t), COLS:COLS + B])
        panel = mm(jnp.concatenate([k_high, k_low, k_high], axis=1), right_w[...])
        panels[rows_of(t), :] = panel
        p_high, p_low = split2(panel)
        left_p[rows_of(t), 0:B] = p_high
        left_p[rows_of(t), B:2 * B] = p_low
        left_p[rows_of(t), 2 * B:3 * B] = p_high
        panel_copy(t).start()

    loop(0, STEPS, panel_tile)

    def out_copy(t, slot, i):
        span = pl.ds(CHUNK * i, CHUNK)
        return pltpu.make_async_copy(
            outs.at[slot, :, span], out_hbm.at[rows_of(t), span], out_sem.at[slot, i]
        )

    def main(t):
        slot = t % 2
        for i in range(COLS // CHUNK):
            @pl.when(t >= 2)
            def _():
                out_copy(t - 2, slot, i).wait()

            span = slice(CHUNK * i, CHUNK * (i + 1))
            outs[slot, :, span] = k_ref[rows_of(t), span] - mm(left_p[rows_of(t), :], right_p[:, span])
            out_copy(t, slot, i).start()

    loop(0, STEPS, main)
    loop(0, STEPS, lambda t: panel_copy(t).wait())
    for t in (STEPS - 2, STEPS - 1):
        for i in range(COLS // CHUNK):
            out_copy(t, t % 2, i).wait()


def apply_panel(k, k_pc, w):
    vmem = pl.BlockSpec(memory_space=pltpu.VMEM)
    hbm = pl.BlockSpec(memory_space=pltpu.HBM)
    dma = pltpu.SemaphoreType.DMA
    n = N_COL * OWN
    return pl.pallas_call(
        apply_kernel,
        out_shape=(jax.ShapeDtypeStruct((n, COLS), F32), jax.ShapeDtypeStruct((n, B), F32)),
        in_specs=[vmem, vmem, vmem],
        out_specs=(hbm, hbm),
        scratch_shapes=[
            pltpu.VMEM((3 * B, COLS), BF16),
            pltpu.VMEM((3 * B, B), BF16),
            pltpu.VMEM((n, 3 * B), BF16),
            pltpu.VMEM((n, B), F32),
            pltpu.VMEM((2, TILE, COLS), F32),
            dma((2, COLS // CHUNK)), dma((STEPS,)),
        ],
        compiler_params=pltpu.CompilerParams(vmem_limit_bytes=28 * 1024 * 1024),
        cost_estimate=pl.CostEstimate(flops=8 * 10**9, bytes_accessed=25 * 10**6, transcendentals=0),
    )(k, k_pc, w)


def local(features, squared_scales, noise_var, signal):
    hbm = lambda a: pltpu.with_memory_space_constraint(a, pltpu.HBM)
    k, k_pc, w = build(
        hbm(features),
        hbm(noise_var.reshape(1, OWN)),
        hbm(squared_scales.reshape(1, F)),
        signal.reshape(1, 1),
    )
    return apply_panel(*(pltpu.with_memory_space_constraint(a, pltpu.VMEM) for a in (k, k_pc, w)))


def solution(mesh):
    return jax.shard_map(
        local,
        mesh=mesh,
        in_specs=(P(("row", "col"), None), P(), P(("row", "col")), P()),
        out_specs=(P("row", "col"), P("row", None)),
        check_vma=False,
    )
```

time: 64.4 us -> 62.4 us (0.969)
  the two profiles are of different devices: /device:TPU:41 before, /device:TPU:7 now
where the time goes in v1:
time: 62.4 us; the launch traced here: 62.3 us
  Pallas kernels  61 us (98%)
  between operations  1.28 us (2%)
    pallas_call x1, Pallas kernels, build(): pl.pallas_call(build_kernel, out_shape=(pltpu.VMEM((N_COL * OWN, COLS + B...  45.2 us
    pallas_call x1, Pallas kernels, apply_panel(): pl.pallas_call(apply_kernel, out_shape=(jax.ShapeDtypeStruct((n, COLS), F...  15.8 us

profile of v1, /device:TPU:7, one launch (start us, length us, event | category | flops | bytes accessed | tf_op | source)
XLA Modules:
  0.0 62.3 jit_solution(14946161095257271177)
XLA Ops:
  1.3 45.2 %shard_map.59 = (f32[3072,1792]{1,0:T(8,128)S(1)}, f32[256,1536]{1,0:T(8,128)S(1)}, f32[256,256]{1,0:T(8,128)S(1)}) custom-call(f32[192,128]{1,0:T(8,128)} %feat_hbm.1, f32[1,192]{1,0:T(1,128)} %bitcast.4, f32[1,128]{1,0:T(1,128)} %bitcast.5, f32[1,1]{1,0:T(1,128)} %bitcast.3.signal_ref), custom_call_target="tpu_custom_call" | custom-call | flops 1000000000 | bytes 10000000 | tf_op jit(solution)/shard_map/pallas_call | solution.py:525
  46.5 15.8 %shard_map.60 = (f32[3072,1536]{1,0:T(8,128)}, f32[3072,256]{1,0:T(8,128)}) custom-call(f32[3072,1792]{1,0:T(8,128)S(1)} %get-tuple-element.5.k_ref, f32[256,1536]{1,0:T(8,128)S(1)} %get-tuple-element.6.k_pc_ref, f32[256,256]{1,0:T(8,128)S(1)} %get-tuple-element.7.w_ref), custom_call_target="tpu_custom_call" | custom-call | flops 8000000000 | bytes 25000000 | tf_op jit(solution)/shard_map/pallas_call | solution.py:624

commit v2 on v1

--- a/solution.py
+++ b/solution.py
@@ -18,10 +18,14 @@
 N_COL = 16
 NB = 32
 TILE = 384
+PT = 1536
+PARTS = 1
+MC = 512
 STEPS = 8
 COLS = 1536
 HALF = 96
 CHUNK = 512
+W_AT = (1, 3)
 SPANS = ((0, 512), (512, 1024), (1024, 1536), (1536, 1792))
 FOLD = math.sqrt(5.0) / math.log(2.0)
 LN2 = math.log(2.0)
@@ -81,10 +85,11 @@
 
 
 def matern(u2, signal):
+    start = jnp.log2(jnp.full((1, 1), LN2 * LN2 / 3.0, F32) * signal)
     a = jnp.maximum(u2, 1e-30)
     u = a * lax.rsqrt(a)
-    poly = signal + u * (signal * LN2 + u * (signal * (LN2 * LN2 / 3.0)))
-    return poly * jnp.exp2(-u)
+    v = u + 1.5 / LN2
+    return (v * v + 0.75 / (LN2 * LN2)) * jnp.exp2(start - u)
 
 
 def pivot_noise(tile0, tile1):
@@ -111,13 +116,14 @@
 def eliminate(aug, w_ref, between):
     sub8 = lax.broadcasted_iota(jnp.int32, (8, F), 0)
 
-    def block_step(step):
+    def block_step(step, half):
         between(step)
         base = pl.multiple_of(step * NB, NB)
-        half = step // 4
         shift = lax.rem(F - NB * lax.rem(step, 4), F)
-        group = aug[pl.ds(base, NB), pl.ds(pl.multiple_of(half * F, F), F)]
-        group = pltpu.roll(group, shift, 1)
+        width = 3 * F
+        span = slice(half * F, half * F + width)
+        panel = [aug[pl.ds(base + 8 * g, 8), span] for g in range(4)]
+        group = pltpu.roll(jnp.concatenate([part[:, 0:F] for part in panel], axis=0), shift, 1)
         rep = [
             [
                 jnp.broadcast_to(group[8 * g:8 * g + 8, i:i + 1], (8, F)) if g >= i // 8 else None
@@ -125,7 +131,6 @@
             ]
             for i in range(NB)
         ]
-        panel = [aug[pl.ds(base + 8 * g, 8), :] for g in range(4)]
         root = []
         for j in range(NB):
             gj, sj = divmod(j, 8)
@@ -138,25 +143,32 @@
                 entry = jnp.broadcast_to(rep[j][gi][si:si + 1, :], (8, F))
                 for g in range(gi, 4):
                     rep[i][g] = rep[i][g] - entry * mult[g]
-            line = jnp.broadcast_to(panel[gj][sj:sj + 1, :], (8, 2 * B))
+            line = jnp.broadcast_to(panel[gj][sj:sj + 1, :], (8, width))
             for g in range(gj, 4):
                 factor = mult[g]
                 if g == gj:
                     factor = jnp.where(sub8 > sj, factor, 0.0)
-                panel[g] = panel[g] - jnp.concatenate([factor] * 4, axis=1) * line
+                panel[g] = panel[g] - jnp.concatenate([factor] * 3, axis=1) * line
         out = []
         for g in range(4):
             scale_rows = root[8 * g]
             for s in range(1, 8):
                 scale_rows = jnp.where(sub8 == s, root[8 * g + s], scale_rows)
-            out.append(panel[g] * jnp.concatenate([scale_rows] * 4, axis=1))
+            out.append(panel[g] * jnp.concatenate([scale_rows] * 3, axis=1))
         block = jnp.concatenate(out, axis=0)
-        w_ref[pl.ds(base, NB), :] = block[:, B:2 * B]
-        aug[...] -= jnp.dot(
-            block[:, 0:B].T, block, precision=lax.Precision.HIGHEST, preferred_element_type=F32
+        if half == 0:
+            w_ref[pl.ds(base, NB), 0:F] = block[:, 2 * F:3 * F]
+            w_ref[pl.ds(base, NB), F:B] = jnp.zeros((NB, F), F32)
+            left = block[:, 0:B]
+        else:
+            w_ref[pl.ds(base, NB), :] = block[:, F:3 * F]
+            left = block[:, 0:F]
+        aug[half * F:B, span] -= jnp.dot(
+            left.T, block, precision=lax.Precision.HIGHEST, preferred_element_type=F32
         )
 
-    loop(0, B // NB, block_step)
+    loop(0, 4, lambda step: block_step(step, 0))
+    loop(4, 8, lambda step: block_step(step, 1))
 
 
 def build_kernel(
@@ -307,14 +319,21 @@
 
         loop(1, 4, go)
 
+    def rest_of_rows():
+        for i in (1, 3, 2):
+            wait_top(x_at(i))
+            wait_bottom(y_at(i))
+            second_go(i)
+
+    def rest_of_columns():
+        for k in (1, 3, 2):
+            z_copy(k, (z + k) % 4).wait_recv()
+            xy_go(k)
+
+    loop(1, 4, lambda k: z_copy(k, z).start())
     loop(1, 4, first_go)
-    loop(1, 4, lambda k: z_copy(k, z).start())
     xy_go(0)
     second_go(0)
-    for i in (1, 3, 2):
-        wait_top(x_at(i))
-        wait_bottom(y_at(i))
-        second_go(i)
 
     def s2_copy(k):
         return remote(piv_ref.at[c], piv_ref.at[c], s2_send.at[k], s2_recv, k, c)
@@ -326,16 +345,6 @@
     @pl.when(r == 0)
     def _():
         loop(1, N_ROW, lambda k: s2_copy(k).start())
-
-    def z_then_xy(k):
-        z_copy(k, (z + k) % 4).wait_recv()
-        xy_go(k)
-
-    loop(1, 4, z_then_xy)
-
-    @pl.when(r != 0)
-    def _():
-        s2_copy(0).wait_recv()
 
     def peer(k):
         return ((x + k // 4) % 4) * 4 + (y + k % 4) % 4
@@ -345,7 +354,9 @@
             piv_ref.at[slot], piv_ref.at[slot], s3_send.at[k], s3_recv.at[slot], r, peer(k)
         )
 
-    loop(1, N_COL, lambda k: s3_copy(k, c).start())
+    @pl.when(r == 0)
+    def _():
+        loop(1, N_COL, lambda k: s3_copy(k, c).start())
 
     def sib_copy(i):
         return remote(cols_ref.at[i], cols_ref.at[i], sib_send.at[i], cols_recv.at[i], sib, c)
@@ -393,16 +404,29 @@
         aug[:, B:2 * B] = jnp.where(eye(B), 1.0, 0.0)
 
         def between(step):
+            @pl.when(step == 2)
+            def _():
+                rest_of_columns()
+
             @pl.when(step == 5)
             def _():
                 loop(0, 4, hand_over)
+                rest_of_rows()
 
         eliminate(aug, w_ref, between)
         loop(1, N_COL, lambda p: w1_copy(p).start())
 
     @pl.when(jnp.logical_not(root))
     def _():
+        rest_of_columns()
+
+        @pl.when(r != 0)
+        def _():
+            s2_copy(0).wait_recv()
+            loop(1, N_COL, lambda k: s3_copy(k, c).start())
+
         loop(0, 4, hand_over)
+        rest_of_rows()
 
     loop(1, N_COL, lambda k: s3_copy(k, peer(k)).wait_recv())
     loop(0, 4, lambda k: wait_cols(2 * k + 1 - core))
@@ -422,9 +446,11 @@
     left_d[:, 3 * F:4 * F] = left_ones(TILE)
 
     def tile(k):
-        t = (c // 2 + k) % STEPS
-
-        @pl.when((k == 2) & (r == 0))
+        turn = k // 2
+        turn = turn + turn // 2 - 2 * (turn // 3)
+        t = 2 * ((x + turn) % 4) + (y // 2 + k) % 2
+
+        @pl.when((k == W_AT[0]) & (r == 0))
         def _():
             @pl.when(c != 0)
             def _():
@@ -433,7 +459,7 @@
             loop(1, N_ROW, lambda to: w2_copy(to).start())
             loop(1, N_COL, w3_go)
 
-        @pl.when((k == 4) & (r != 0))
+        @pl.when((k == W_AT[1]) & (r != 0))
         def _():
             w2_copy(0).wait_recv()
             loop(1, N_COL, w3_go)
@@ -575,44 +601,51 @@
         right_p[B:2 * B, span] = p_high
         right_p[2 * B:3 * B, span] = p_low
 
+    def prow(t):
+        return pl.ds(pl.multiple_of(t * PT, PT), PT)
+
     def panel_copy(t):
         return pltpu.make_async_copy(
-            panels.at[rows_of(t), :], panel_hbm.at[rows_of(t), :], panel_sem.at[t]
+            panels.at[prow(t), :], panel_hbm.at[prow(t), :], panel_sem.at[t]
         )
 
     def panel_tile(t):
-        k_high, k_low = split2(k_ref[rows_of(t), COLS:COLS + B])
+        k_high, k_low = split2(k_ref[prow(t), COLS:COLS + B])
         panel = mm(jnp.concatenate([k_high, k_low, k_high], axis=1), right_w[...])
-        panels[rows_of(t), :] = panel
+        panels[prow(t), :] = panel
         p_high, p_low = split2(panel)
-        left_p[rows_of(t), 0:B] = p_high
-        left_p[rows_of(t), B:2 * B] = p_low
-        left_p[rows_of(t), 2 * B:3 * B] = p_high
+        left_p[prow(t), 0:B] = p_high
+        left_p[prow(t), B:2 * B] = p_low
+        left_p[prow(t), 2 * B:3 * B] = p_high
         panel_copy(t).start()
 
-    loop(0, STEPS, panel_tile)
+    loop(0, 3072 // PT, panel_tile)
 
     def out_copy(t, slot, i):
-        span = pl.ds(CHUNK * i, CHUNK)
+        part = TILE // PARTS
+        rows = pl.ds(pl.multiple_of(t * TILE + part * i, 8), part)
         return pltpu.make_async_copy(
-            outs.at[slot, :, span], out_hbm.at[rows_of(t), span], out_sem.at[slot, i]
+            outs.at[slot, pl.ds(part * i, part), :], out_hbm.at[rows, :], out_sem.at[slot, i]
         )
 
     def main(t):
         slot = t % 2
-        for i in range(COLS // CHUNK):
-            @pl.when(t >= 2)
-            def _():
+
+        @pl.when(t >= 2)
+        def _():
+            for i in range(PARTS):
                 out_copy(t - 2, slot, i).wait()
 
-            span = slice(CHUNK * i, CHUNK * (i + 1))
+        for i in range(COLS // MC):
+            span = slice(MC * i, MC * (i + 1))
             outs[slot, :, span] = k_ref[rows_of(t), span] - mm(left_p[rows_of(t), :], right_p[:, span])
+        for i in range(PARTS):
             out_copy(t, slot, i).start()
 
     loop(0, STEPS, main)
-    loop(0, STEPS, lambda t: panel_copy(t).wait())
+    loop(0, 3072 // PT, lambda t: panel_copy(t).wait())
     for t in (STEPS - 2, STEPS - 1):
-        for i in range(COLS // CHUNK):
+        for i in range(PARTS):
             out_copy(t, t % 2, i).wait()
 
 
@@ -632,7 +665,7 @@
             pltpu.VMEM((n, 3 * B), BF16),
             pltpu.VMEM((n, B), F32),
             pltpu.VMEM((2, TILE, COLS), F32),
-            dma((2, COLS // CHUNK)), dma((STEPS,)),
+            dma((2, PARTS)), dma((STEPS,)),
         ],
         compiler_params=pltpu.CompilerParams(vmem_limit_bytes=28 * 1024 * 1024),
         cost_estimate=pl.CostEstimate(flops=8 * 10**9, bytes_accessed=25 * 10**6, transcendentals=0),

time: 62.4 us -> 56.3 us (0.902); the launches traced: 62.3 us -> 55.4 us
  Pallas kernels: 61 us -> 54.1 us
    pallas_call x1, Pallas kernels: 45.2 us -> 40.6 us  [build(): pl.pallas_call(build_kernel, out_shape=(pltpu.VMEM((N_COL * OWN, COLS + B...]
    pallas_call x1, Pallas kernels: 15.8 us -> 13.5 us  [apply_panel(): pl.pallas_call(apply_kernel, out_shape=(jax.ShapeDtypeStruct((n, COLS), F...]
where the time goes in v2:
time: 56.3 us; the launch traced here: 55.4 us
  Pallas kernels  54.1 us (96%)
  between operations  1.28 us (2%)
    pallas_call x1, Pallas kernels, build(): pl.pallas_call(build_kernel, out_shape=(pltpu.VMEM((N_COL * OWN, COLS + B...  40.6 us
    pallas_call x1, Pallas kernels, apply_panel(): pl.pallas_call(apply_kernel, out_shape=(jax.ShapeDtypeStruct((n, COLS), F...  13.5 us

profile of v2, /device:TPU:7, one launch (start us, length us, event | category | flops | bytes accessed | tf_op | source)
XLA Modules:
  0.0 55.4 jit_solution(18426225276346310326)
XLA Ops:
  1.3 40.6 %shard_map.59 = (f32[3072,1792]{1,0:T(8,128)S(1)}, f32[256,1536]{1,0:T(8,128)S(1)}, f32[256,256]{1,0:T(8,128)S(1)}) custom-call(f32[192,128]{1,0:T(8,128)} %feat_hbm.1, f32[1,192]{1,0:T(1,128)} %bitcast.4, f32[1,128]{1,0:T(1,128)} %bitcast.5, f32[1,1]{1,0:T(1,128)} %bitcast.3.signal_ref), custom_call_target="tpu_custom_call" | custom-call | flops 1000000000 | bytes 10000000 | tf_op jit(solution)/shard_map/pallas_call | solution.py:551
  41.9 13.5 %shard_map.60 = (f32[3072,1536]{1,0:T(8,128)}, f32[3072,256]{1,0:T(8,128)}) custom-call(f32[3072,1792]{1,0:T(8,128)S(1)} %get-tuple-element.5.k_ref, f32[256,1536]{1,0:T(8,128)S(1)} %get-tuple-element.6.k_pc_ref, f32[256,256]{1,0:T(8,128)S(1)} %get-tuple-element.7.w_ref), custom_call_target="tpu_custom_call" | custom-call | flops 8000000000 | bytes 25000000 | tf_op jit(solution)/shard_map/pallas_call | solution.py:657

commit v3 on v2

--- a/solution.py
+++ b/solution.py
@@ -25,7 +25,7 @@
 COLS = 1536
 HALF = 96
 CHUNK = 512
-W_AT = (1, 3)
+W_AT = (2, 4)
 SPANS = ((0, 512), (512, 1024), (1024, 1536), (1536, 1792))
 FOLD = math.sqrt(5.0) / math.log(2.0)
 LN2 = math.log(2.0)
@@ -211,7 +211,12 @@
 
     loop(1, N_COL, lambda k: signal_to(r, (c + k) % N_COL))
     loop(1, 4, greet_z)
-    loop(0, N_COL, lambda k: signal_to(sib, (c + k) % N_COL))
+    signal_to(sib, c)
+
+    @pl.when((c // 2) % 2 != core)
+    def _():
+        loop(0, 4, lambda i: signal_to(sib, c % 2 * 8 + 2 * i + core))
+
 
     for copy in in_copies:
         copy.wait()
@@ -226,7 +231,13 @@
             stage[q, 0:16, :] = zbuf[z, 16 * q:16 * q + 16, :]
             stage[q, 16:PIECE, :] = tile
 
-    pl.semaphore_wait(barrier, 15 + 16 + 6)
+    @pl.when(index % 2 != core)
+    def _():
+        pl.semaphore_wait(barrier, 15 + 6 + 1 + 4)
+
+    @pl.when(index % 2 == core)
+    def _():
+        pl.semaphore_wait(barrier, 15 + 6 + 1)
 
     tail_copy = remote(stage.at[pl.ds(0, 4)], tail, tail_send, tail_recv, 0, 0)
 
@@ -319,8 +330,8 @@
 
         loop(1, 4, go)
 
-    def rest_of_rows():
-        for i in (1, 3, 2):
+    def rest_of_rows(order=(1, 3, 2)):
+        for i in order:
             wait_top(x_at(i))
             wait_bottom(y_at(i))
             second_go(i)
@@ -342,7 +353,7 @@
     def _():
         s1_copy(0, c).wait_recv()
 
-    @pl.when(r == 0)
+    @pl.when((r == 0) & (c != 0))
     def _():
         loop(1, N_ROW, lambda k: s2_copy(k).start())
 
@@ -354,7 +365,7 @@
             piv_ref.at[slot], piv_ref.at[slot], s3_send.at[k], s3_recv.at[slot], r, peer(k)
         )
 
-    @pl.when(r == 0)
+    @pl.when((r == 0) & (c != 0))
     def _():
         loop(1, N_COL, lambda k: s3_copy(k, c).start())
 
@@ -404,6 +415,11 @@
         aug[:, B:2 * B] = jnp.where(eye(B), 1.0, 0.0)
 
         def between(step):
+            @pl.when(step == 1)
+            def _():
+                loop(1, N_ROW, lambda k: s2_copy(k).start())
+                loop(1, N_COL, lambda k: s3_copy(k, c).start())
+
             @pl.when(step == 2)
             def _():
                 rest_of_columns()
@@ -425,8 +441,9 @@
             s2_copy(0).wait_recv()
             loop(1, N_COL, lambda k: s3_copy(k, c).start())
 
+        rest_of_rows((1,))
         loop(0, 4, hand_over)
-        rest_of_rows()
+        rest_of_rows((3, 2))
 
     loop(1, N_COL, lambda k: s3_copy(k, peer(k)).wait_recv())
     loop(0, 4, lambda k: wait_cols(2 * k + 1 - core))

time: 56.3 us -> 56.1 us (level)
  no operation moved by 1% of the time
where the time goes in v3:
time: 56.1 us; the launch traced here: 55.6 us
  Pallas kernels  54.3 us (97%)
  between operations  1.28 us (2%)
    pallas_call x1, Pallas kernels, build(): pl.pallas_call(build_kernel, out_shape=(pltpu.VMEM((N_COL * OWN, COLS + B...  40.8 us
    pallas_call x1, Pallas kernels, apply_panel(): pl.pallas_call(apply_kernel, out_shape=(jax.ShapeDtypeStruct((n, COLS), F...  13.5 us

profile of v3, /device:TPU:7, one launch (start us, length us, event | category | flops | bytes accessed | tf_op | source)
XLA Modules:
  0.0 55.6 jit_solution(871028570681392223)
XLA Ops:
  1.3 40.8 %shard_map.59 = (f32[3072,1792]{1,0:T(8,128)S(1)}, f32[256,1536]{1,0:T(8,128)S(1)}, f32[256,256]{1,0:T(8,128)S(1)}) custom-call(f32[192,128]{1,0:T(8,128)} %feat_hbm.1, f32[1,192]{1,0:T(1,128)} %bitcast.4, f32[1,128]{1,0:T(1,128)} %bitcast.5, f32[1,1]{1,0:T(1,128)} %bitcast.3.signal_ref), custom_call_target="tpu_custom_call" | custom-call | flops 1000000000 | bytes 10000000 | tf_op jit(solution)/shard_map/pallas_call | solution.py:568
  42.1 13.5 %shard_map.60 = (f32[3072,1536]{1,0:T(8,128)}, f32[3072,256]{1,0:T(8,128)}) custom-call(f32[3072,1792]{1,0:T(8,128)S(1)} %get-tuple-element.5.k_ref, f32[256,1536]{1,0:T(8,128)S(1)} %get-tuple-element.6.k_pc_ref, f32[256,256]{1,0:T(8,128)S(1)} %get-tuple-element.7.w_ref), custom_call_target="tpu_custom_call" | custom-call | flops 8000000000 | bytes 25000000 | tf_op jit(solution)/shard_map/pallas_call | solution.py:674
